TPU v7x, 32 devices: a whole 2x2x4 slice. The times are simulated.
32 devices in a mesh: dp: 8 (over z, y), tp: 4 (over x, core).
Axes of the slice: x: 2, y: 2, z: 4, core: 2. Of those that a mesh axis runs over, the one named last changes fastest.
Arguments:
- inputs: bfloat16 [32, 896, 512], P('dp', 'tp'), may hold values from -6 to 6
- dataset: int32 [32], P('dp'), may hold values from 0 to 3, as said below
- variate_mask: int32 [32, 896], P('dp'), may hold values from 0 to 1, as said below
- dataset_bias: bfloat16 [4, 512], replicated, may hold values from -3 to 3
- w_qkv: bfloat16 [3, 512, 512], P(None, None, 'tp'), may hold values from -0.25 to 0.25
- qv_bias: bfloat16 [2, 512], P(None, 'tp'), may hold values from -1.796875 to 1.796875
- w_out: bfloat16 [512, 512], P('tp'), may hold values from -1 to 1
- out_bias: bfloat16 [2, 512], replicated, may hold values from -1.796875 to 1.796875
- w_up: bfloat16 [512, 2048], P(None, 'tp'), may hold values from -0.25 to 0.25
- up_bias: bfloat16 [2048], P('tp'), may hold values from -1.796875 to 1.796875
- w_down: bfloat16 [2048, 512], P('tp'), may hold values from -0.125 to 0.125
- norm_gain: bfloat16 [2, 512], replicated, may hold values from 0.25 to 1.75
- norm_shift: bfloat16 [2, 512], replicated, may hold values from -1.796875 to 1.796875
- cotangent: bfloat16 [32, 896, 512], P('dp', 'tp'), may hold values from -6 to 6
Outputs:
- outputs: bfloat16 [32, 896, 512], P('dp', 'tp')
- input_grad: bfloat16 [32, 896, 512], P('dp', 'tp')
- dataset_bias_grad: float32 [4, 512], replicated
- w_qkv_grad: float32 [3, 512, 512], P(None, None, 'tp')
- qv_bias_grad: float32 [2, 512], P(None, 'tp')
- w_out_grad: float32 [512, 512], P('tp')
- out_bias_grad: float32 [2, 512], replicated
- w_up_grad: float32 [512, 2048], P(None, 'tp')
- up_bias_grad: float32 [2048], P('tp')
- w_down_grad: float32 [2048, 512], P('tp')
- norm_gain_grad: float32 [2, 512], replicated
- norm_shift_grad: float32 [2, 512], replicated
Inputs may be any that keep to these rules, and one draw needn't show every extreme that they name: In every aligned block of 4 windows (those of one index of dp) at least one window has dataset 3. `variate_mask`: variate 0 of every window is live. A window of dataset c has no live variate at or past entry c of (max(1, 7), max(1, 21), max(1, 321), max(1, 862)).
All inputs are finite; a program needn't handle non-finite values.
Results may differ from a plain program's by a relative error of at most 0.017.
Values may be sent and summed in bfloat16 or wider, within the bound.
A program may use at most 128 MiB of HBM per device.

v0:
```python
import math
import jax
import jax.numpy as jnp
from jax import lax
from jax.sharding import PartitionSpec as P

HD = 64
EPSILON = 1e-05
HIGHEST = lax.Precision.HIGHEST
NEG_FILL = -1e30


def layer_forward_norm(residual, gains, shifts):
    center = residual - jnp.mean(residual, axis=-1, keepdims=True)
    factor = lax.rsqrt(jnp.mean(center * center, axis=-1, keepdims=True) + EPSILON)
    normed = center * factor
    return (normed * gains + shifts, normed, factor)


def layer_back_norm(upstream, normed, factor, gains):
    scaled = upstream * gains
    result = factor * (
        scaled
        - jnp.mean(scaled, axis=-1, keepdims=True)
        - normed * jnp.mean(scaled * normed, axis=-1, keepdims=True)
    )
    return (result, jnp.sum(upstream * normed, axis=(0, 1)), jnp.sum(upstream, axis=(0, 1)))


def masked_scores(queries, key_rows, live_row):
    length = queries.shape[0]
    head_count = queries.shape[1] // HD
    q_heads = queries.reshape(length, head_count, HD)
    k_heads = key_rows.reshape(length, head_count, HD)
    scores = jnp.einsum("qhe,khe->hqk", q_heads, k_heads, preferred_element_type=jnp.float32) * (
        1.0 / math.sqrt(HD)
    )
    return (jnp.where(live_row[None, None, :] > 0.5, scores, NEG_FILL), q_heads, k_heads)


def attend_window(packed):
    queries, key_rows, value_rows, live_row = packed
    length = queries.shape[0]
    head_count = queries.shape[1] // HD
    scores, q_heads, k_heads = masked_scores(queries, key_rows, live_row)
    row_top = jnp.max(scores, axis=-1, keepdims=True)
    exponent = jnp.exp(scores - row_top)
    row_total = jnp.sum(exponent, axis=-1, keepdims=True)
    attn_prob = (exponent / row_total).astype(jnp.bfloat16)
    v_heads = value_rows.reshape(length, head_count, HD)
    mixture = jnp.einsum("hqk,khe->qhe", attn_prob, v_heads, preferred_element_type=jnp.float32)
    log_total = (row_top + jnp.log(row_total))[..., 0]
    return (mixture.reshape(length, head_count * HD).astype(jnp.bfloat16), log_total)


def attend_back(packed):
    queries, key_rows, value_rows, live_row, grad_out, log_total = packed
    length = queries.shape[0]
    head_count = queries.shape[1] // HD
    scores, q_heads, k_heads = masked_scores(queries, key_rows, live_row)
    attn_prob = jnp.exp(scores - log_total[..., None])
    prob_low = attn_prob.astype(jnp.bfloat16)
    v_heads = value_rows.reshape(length, head_count, HD)
    grad_heads = grad_out.reshape(length, head_count, HD)
    grad_values = jnp.einsum(
        "hqk,qhe->khe", prob_low, grad_heads, preferred_element_type=jnp.float32
    )
    grad_probs = jnp.einsum("qhe,khe->hqk", grad_heads, v_heads, preferred_element_type=jnp.float32)
    grad_scores = attn_prob * (grad_probs - jnp.sum(attn_prob * grad_probs, axis=-1, keepdims=True))
    score_low = grad_scores.astype(jnp.bfloat16)
    score_scale = 1.0 / math.sqrt(HD)
    grad_queries = (
        jnp.einsum("hqk,khe->qhe", score_low, k_heads, preferred_element_type=jnp.float32)
        * score_scale
    )
    grad_keys = (
        jnp.einsum("hqk,qhe->khe", score_low, q_heads, preferred_element_type=jnp.float32)
        * score_scale
    )
    joined = jnp.concatenate(
        [
            grad_queries.reshape(length, head_count * HD),
            grad_keys.reshape(length, head_count * HD),
            grad_values.reshape(length, head_count * HD),
        ],
        axis=-1,
    )
    return joined.astype(jnp.bfloat16)


def attention_forward(gathered, w_cat, b_cat, w_out, live_full):
    projected = (
        jnp.einsum("wvd,de->wve", gathered, w_cat, preferred_element_type=jnp.float32) + b_cat
    ).astype(jnp.bfloat16)
    col_width = w_out.shape[0]
    mixture, log_total = lax.map(
        attend_window,
        (
            projected[..., :col_width],
            projected[..., col_width : 2 * col_width],
            projected[..., 2 * col_width :],
            live_full,
        ),
    )
    part_sum = jnp.einsum("wvh,hd->wvd", mixture, w_out, preferred_element_type=jnp.float32)
    return (part_sum, projected, mixture, log_total)


def attention_back(grad_rows, gathered, projected, mixture, log_total, live_full, w_cat, w_out):
    w_out_g = jnp.einsum("wvh,wvd->hd", mixture, grad_rows, preferred_element_type=jnp.float32)
    grad_mixture = jnp.einsum(
        "wvd,hd->wvh", grad_rows, w_out, preferred_element_type=jnp.float32
    ).astype(jnp.bfloat16)
    col_width = w_out.shape[0]
    grad_proj = lax.map(
        attend_back,
        (
            projected[..., :col_width],
            projected[..., col_width : 2 * col_width],
            projected[..., 2 * col_width :],
            live_full,
            grad_mixture,
            log_total,
        ),
    )
    w_cat_g = jnp.einsum("wvd,wve->de", gathered, grad_proj, preferred_element_type=jnp.float32)
    b_cat_g = jnp.sum(grad_proj, axis=(0, 1), dtype=jnp.float32)
    part_sum = jnp.einsum("wve,de->wvd", grad_proj, w_cat, preferred_element_type=jnp.float32)
    return (part_sum, w_cat_g, b_cat_g, w_out_g)


def feed_forward(gathered, w_up, up_bias, w_down):
    pre_act = jnp.einsum(
        "wvd,df->wvf", gathered, w_up, preferred_element_type=jnp.float32
    ) + up_bias.astype(jnp.float32)
    act_full, gelu_back = jax.vjp(jax.nn.gelu, pre_act)
    act_low = act_full.astype(jnp.bfloat16)
    part_sum = jnp.einsum("wvf,fd->wvd", act_low, w_down, preferred_element_type=jnp.float32)
    return (part_sum, act_low, gelu_back)


def feed_back(grad_rows, gathered, act_low, gelu_back, w_up, w_down):
    w_down_g = jnp.einsum("wvf,wvd->fd", act_low, grad_rows, preferred_element_type=jnp.float32)
    grad_act = jnp.einsum("wvd,fd->wvf", grad_rows, w_down, preferred_element_type=jnp.float32)
    grad_pre = gelu_back(grad_act)[0]
    up_bias_g = jnp.sum(grad_pre, axis=(0, 1))
    grad_low = grad_pre.astype(jnp.bfloat16)
    w_up_g = jnp.einsum("wvd,wvf->df", gathered, grad_low, preferred_element_type=jnp.float32)
    part_sum = jnp.einsum("wvf,df->wvd", grad_low, w_up, preferred_element_type=jnp.float32)
    return (part_sum, w_up_g, up_bias_g, w_down_g)


def shards(
    inputs,
    dataset,
    variate_mask,
    dataset_bias,
    w_qkv,
    qv_bias,
    w_out,
    out_bias,
    w_up,
    up_bias,
    w_down,
    norm_gain,
    norm_shift,
    cotangent,
):
    my_rank = lax.axis_index("tp")
    one_hot = (
        dataset[:, None] == jnp.arange(dataset_bias.shape[0], dtype=jnp.int32)[None, :]
    ).astype(jnp.float32)
    offsets = jnp.dot(one_hot, dataset_bias.astype(jnp.float32), precision=HIGHEST)
    gains = norm_gain.astype(jnp.float32)
    shifts = norm_shift.astype(jnp.float32)
    biases = out_bias.astype(jnp.float32)
    rows_in, cot_in = (inputs, cotangent)
    qkv_used, qvb_used, out_used, up_used, upb_used, down_used = (
        w_qkv,
        qv_bias,
        w_out,
        w_up,
        up_bias,
        w_down,
    )
    row_start = my_rank * inputs.shape[1]
    row_span = rows_in.shape[1]
    win_live = variate_mask.astype(jnp.float32)
    live_rows = lax.dynamic_slice_in_dim(win_live, row_start, row_span, 1)
    col_width = out_used.shape[0]
    model_width = qkv_used.shape[1]
    w_cat = jnp.transpose(qkv_used, (1, 0, 2)).reshape(model_width, 3 * col_width)
    b_cat = jnp.concatenate(
        [
            qvb_used[0].astype(jnp.float32),
            jnp.zeros((col_width,), jnp.float32),
            qvb_used[1].astype(jnp.float32),
        ]
    )
    base_rows = rows_in.astype(jnp.float32) + offsets[:, None, :]
    act_in = base_rows.astype(jnp.bfloat16)
    act_full = lax.all_gather(act_in, "tp", axis=1, tiled=True)
    attn_part, projected, mixture, log_total = attention_forward(
        act_full, w_cat, b_cat, out_used, win_live
    )
    attn_sum = lax.psum_scatter(attn_part, "tp", scatter_dimension=1, tiled=True)
    hidden, normed_one, factor_one = layer_forward_norm(
        base_rows + attn_sum + biases[0], gains[0], shifts[0]
    )
    hidden_low = hidden.astype(jnp.bfloat16)
    hidden_full = lax.all_gather(hidden_low, "tp", axis=1, tiled=True)
    ffn_part, act_low, gelu_back = feed_forward(hidden_full, up_used, upb_used, down_used)
    ffn_sum = lax.psum_scatter(
        ffn_part.astype(jnp.bfloat16), "tp", scatter_dimension=1, tiled=True
    ).astype(jnp.float32)
    final_rows, normed_two, factor_two = layer_forward_norm(
        hidden + ffn_sum + biases[1], gains[1], shifts[1]
    )
    result_rows = (final_rows * live_rows[:, :, None]).astype(jnp.bfloat16)
    grad_final = cot_in.astype(jnp.float32) * live_rows[:, :, None]
    grad_two, gain_two, shift_two = layer_back_norm(grad_final, normed_two, factor_two, gains[1])
    grad_two_low = grad_two.astype(jnp.bfloat16)
    grad_two_full = lax.all_gather(grad_two_low, "tp", axis=1, tiled=True)
    ffn_back_part, up_grad, upb_grad, down_grad = feed_back(
        grad_two_full, hidden_full, act_low, gelu_back, up_used, down_used
    )
    ffn_back = lax.psum_scatter(
        ffn_back_part.astype(jnp.bfloat16), "tp", scatter_dimension=1, tiled=True
    ).astype(jnp.float32)
    grad_one, gain_one, shift_one = layer_back_norm(
        grad_two + ffn_back, normed_one, factor_one, gains[0]
    )
    grad_one_low = grad_one.astype(jnp.bfloat16)
    grad_one_full = lax.all_gather(grad_one_low, "tp", axis=1, tiled=True)
    attn_back_part, cat_grad, bcat_grad, out_grad = attention_back(
        grad_one_full, act_full, projected, mixture, log_total, win_live, w_cat, out_used
    )
    attn_back = lax.psum_scatter(
        attn_back_part.astype(jnp.bfloat16), "tp", scatter_dimension=1, tiled=True
    ).astype(jnp.float32)
    grad_base = grad_one + attn_back
    input_low = grad_base.astype(jnp.bfloat16)
    bias_grad = jnp.dot(one_hot.T, jnp.sum(grad_base, axis=1), precision=HIGHEST)
    qkv_grad = jnp.transpose(cat_grad.reshape(model_width, 3, col_width), (1, 0, 2))
    qvb_grad = jnp.stack([bcat_grad[:col_width], bcat_grad[2 * col_width :]])
    weight_totals = lax.psum((qkv_grad, qvb_grad, out_grad, up_grad, upb_grad, down_grad), "dp")
    shared = lax.psum(
        (
            bias_grad,
            jnp.stack([gain_one, gain_two]),
            jnp.stack([shift_one, shift_two]),
            jnp.stack([jnp.sum(grad_one, axis=(0, 1)), jnp.sum(grad_two, axis=(0, 1))]),
        ),
        ("dp", "tp"),
    )
    return (
        result_rows,
        input_low,
        shared[0],
        weight_totals[0],
        weight_totals[1],
        weight_totals[2],
        shared[3],
        weight_totals[3],
        weight_totals[4],
        weight_totals[5],
        shared[1],
        shared[2],
    )


def solution(mesh):
    in_specs = (
        P("dp", "tp", None),
        P("dp"),
        P("dp", None),
        P(),
        P(None, None, "tp"),
        P(None, "tp"),
        P("tp", None),
        P(),
        P(None, "tp"),
        P("tp"),
        P("tp", None),
        P(),
        P(),
        P("dp", "tp", None),
    )
    out_specs = (
        P("dp", "tp", None),
        P("dp", "tp", None),
        P(),
        P(None, None, "tp"),
        P(None, "tp"),
        P("tp", None),
        P(),
        P(None, "tp"),
        P("tp"),
        P("tp", None),
        P(),
        P(),
    )
    return jax.shard_map(shards, mesh=mesh, in_specs=in_specs, out_specs=out_specs, check_vma=False)
```

profile of v0, /device:TPU:0, one launch (start us, length us, event | category | flops | bytes accessed | tf_op | source)
XLA Modules:
  0.0 612.9 jit_solution(5548335376186596348)
XLA Ops:
  8.2 2.3 fusion.29
  13.2 31.6 %all-gather.5.cloned.1.call-done = bf16[4,896,512]{2,1,0:T(8,128)(2,1)} async-done(((bf16[4,224,512]{2,1,0:T(8,128)(2,1)}), bf16[4,896,512]{2,1,0:T(8,128)(2,1)}) %all-gather.5.cloned.1.call-update) | async-done | bytes 3670032 | tf_op jit(solution)/shard_map/all_gather | solution.py:202
  44.8 4.1 add_convert_fusion
  53.3 23.3 %while.22 = (s32[]{:T(128)}, bf16[4,896,128]{1,2,0:T(8,128)(2,1)}, f32[4,2,896]{2,1,0:T(2,128)S(1)}, bf16[4,896,128]{1,2,0:T(8,128)(2,1)S(1)}, f32[4,896]{1,0:T(...) while((s32[]{:T(128)}, bf16[4,896,128]{1,2,0:T(8,128)(2,1)}, ...), condition=%wide.region_3.4_spmd, body=%wide.region_0.3_spmd.sunk | while | flops 430423168 | bytes 22084720 | solution.py:96
  76.6 5.9 fusion.42
  83.3 64.9 %reduce-scatter.5.cloned.1.call-done = f32[4,224,512]{2,1,0:T(8,128)} async-done(((f32[4,896,512]{2,1,0:T(8,128)}), f32[4,224,512]{2,1,0:T(8,128)}) %reduce-scatter.5.cloned.1.call-update) | async-done | bytes 1835024 | tf_op jit(solution)/shard_map/reduce_scatter | solution.py:206
  152.6 31.1 %all-gather.7.cloned.1.call-done = bf16[4,896,512]{2,1,0:T(8,128)(2,1)} async-done(((bf16[4,224,512]{2,1,0:T(8,128)(2,1)}), bf16[4,896,512]{2,1,0:T(8,128)(2,1)}) %all-gather.7.cloned.1.call-update) | async-done | bytes 3670032 | tf_op jit(solution)/shard_map/all_gather | solution.py:211
  183.7 4.2 fusion.39
  188.0 3.0 copy-done.5
  190.9 4.4 convolution_convert_fusion.2
  195.5 41.3 %reduce-scatter.7.cloned.1.call-done = bf16[4,224,512]{2,1,0:T(8,128)(2,1)} async-done(((bf16[4,896,512]{2,1,0:T(8,128)(2,1)}), bf16[4,224,512]{2,1,0:T(8,128)(2,1)}) %reduce-scatter.7.cloned.1.call-update) | async-done | bytes 917520 | tf_op jit(solution)/shard_map/reduce_scatter | solution.py:213
  240.3 2.3 fusion.51
  242.7 31.6 %all-gather.9.cloned.1.call-done = bf16[4,896,512]{2,1,0:T(8,128)(2,1)} async-done(((bf16[4,224,512]{2,1,0:T(8,128)(2,1)}), bf16[4,896,512]{2,1,0:T(8,128)(2,1)}) %all-gather.9.cloned.1.call-update) | async-done | bytes 3670032 | tf_op jit(solution)/shard_map/all_gather | solution.py:223
  274.3 9.2 %fusion.58 = (f32[512]{0:T(512)S(1)}, bf16[4,896,512]{2,1,0:T(8,128)(2,1)S(1)}) fusion(f32[4,896,512]{2,1,0:T(8,128)} %copy-done.5, f32[512]{0:T(512)S(1)} %convert_element_type.131, bf16[4,896,512]{2,1,0:T(8,128)(2,1)} %all-gather.9.cloned.1.call-done, bf16[512,512]{1,0:T(8,128)(2,1)S(1)} %copy-done), kind=kOutput, calls=%fused_computation.123 | convolution fusion | flops 1919417856 | bytes 15208448 | tf_op jit(solution)/shard_map/wvd,fd->wvf/dot_general | solution.py:144
  285.5 4.1 convolution_convert_fusion.1
  289.8 41.2 %reduce-scatter.9.cloned.1.call-done = bf16[4,224,512]{2,1,0:T(8,128)(2,1)} async-done(((bf16[4,896,512]{2,1,0:T(8,128)(2,1)}), bf16[4,224,512]{2,1,0:T(8,128)(2,1)}) %reduce-scatter.9.cloned.1.call-update) | async-done | bytes 917520 | tf_op jit(solution)/shard_map/reduce_scatter | solution.py:227
  331.0 3.0 multiply_reduce_fusion.2
  336.0 31.6 %all-gather.11.cloned.1.call-done = bf16[4,896,512]{2,1,0:T(8,128)(2,1)} async-done(((bf16[4,224,512]{2,1,0:T(8,128)(2,1)}), bf16[4,896,512]{2,1,0:T(8,128)(2,1)}) %all-gather.11.cloned.1.call-update) | async-done | bytes 3670032 | tf_op jit(solution)/shard_map/all_gather | solution.py:234
  367.6 3.1 convolution_convert_fusion.3
  370.8 44.7 %while.23 = (s32[]{:T(128)}, bf16[4,896,384]{1,2,0:T(8,128)(2,1)}, bf16[4,896,128]{1,2,0:T(8,128)(2,1)S(1)}, f32[4,896]{1,0:T(4,128)S(1)}, bf16[4,896,128]{1,2,0...) while((s32[]{:T(128)}, bf16[4,896,384]{1,2,0:T(8,128)(2,1)}, ...), condition=%wide.region_17.18_spmd, body=%wide.region_15.17_spmd.sunk | while | flops 1054325888 | bytes 54190204 | solution.py:115
  377.0 2.2 multiply_convert_fusion.6
  399.4 2.2 multiply_convert_fusion.6
  415.5 5.7 convolution_convert_fusion
  421.5 6.3 %fusion.31 = f32[512,512]{1,0:T(8,128)} fusion(bf16[4,896,512]{2,1,0:T(8,128)(2,1)} %all-gather.7.cloned.1.call-done, bf16[4,896,512]{2,1,0:T(8,128)(2,1)} %copy-done.9), kind=kOutput, calls=%fused_computation.78 | convolution fusion | flops 1879048192 | bytes 8388608 | tf_op jit(solution)/shard_map/wvd,wvf->df/dot_general | solution.py:148
  427.8 8.5 %convolution_bitcast_fusion = f32[512,512]{1,0:T(8,128)} fusion(bf16[4,896,512]{2,1,0:T(8,128)(2,1)S(1)} %copy-done.22, f32[4,896,512]{2,1,0:T(8,128)} %copy-done.5, f32[512]{0:T(512)S(1)} %convert_element_type.131), kind=kOutput, calls=%fused_computation.77 | convolution fusion | flops 1897398272 | bytes 12060672 | tf_op jit(solution)/shard_map/wvf,wvd->fd/dot_general | solution.py:143
  439.1 3.8 convolution_bitcast_fusion.1
  442.9 2.3 convert_reduce_fusion
  445.3 22.0 %all-reduce.1 = (f32[2,128]{1,0:T(2,128)}, f32[512]{0:T(512)}) all-reduce(f32[2,128]{1,0:T(2,128)S(1)} %pad_maximum_fusion.4, f32[512]{0:T(512)S(1)} %get-tuple-element.207), channel_id=1, replica_groups=mesh['dp'=8,'tp'=4] {'dp'}, use_global_device_ids=true, to_apply=%region_23.24 | all-reduce | flops 768 | bytes 6144 | tf_op jit(solution)/shard_map/psum | solution.py:246
  467.3 2.5 fusion.49
  470.1 41.5 %all-reduce = (f32[4,512]{1,0:T(4,128)}, f32[2,512]{1,0:T(2,128)}, f32[2,512]{1,0:T(2,128)}, f32[2,512]{1,0:T(2,128)}) all-reduce(f32[4,512]{1,0:T(4,128)S(1)} %fusion.44, f32[2,512]{1,0:T(2,128)S(1)} %pad_maximum_fusion, f32[2,512]{1,0:T(2,128)S(1)} %pad_maximum_fusion.1, ...), channel_id=1, replica_groups=mesh['dp'=8,'tp'=4] {'dp','tp'}, use_global_device_ids=true, to_apply=%region_20.21 | all-reduce | flops 5120 | bytes 40960 | tf_op jit(solution)/shard_map/psum | solution.py:247
  511.6 87.5 %all-reduce.5.cloned.1.call-done = (f32[3,512,128]{2,1,0:T(8,128)}, f32[128,512]{1,0:T(8,128)}, f32[512,512]{1,0:T(8,128)}, f32[512,512]{1,0:T(8,128)}) async-done(((f32[3,512,128]{2,1,0:T(8,128)}, f32[128,512]{1,0:T(8,128)}, f32[512,512]{1,0:T(8,128)}, f32[512,512]{1,0:T(8,128)}), (f32[3,512,128]{2,1,0:T(8,128)}, f32[128,512]{1,0:T(8,128)}, f32[512,512]{1,0:T(8,128)}, ...) | async-done | bytes 3145744 | tf_op jit(solution)/shard_map/psum | solution.py:246
  602.9 2.3 copy.99
  (191 shorter events, 92.1 us)
Async XLA Ops:
  7.2 183.8 %copy-start = (bf16[512,512]{1,0:T(8,128)(2,1)S(1)}, bf16[512,512]{1,0:T(8,128)(2,1)}, u32[]{:S(2)}) copy-start(bf16[512,512]{1,0:T(8,128)(2,1)} %param.28) | copy-start | bytes 1572868
  7.2 37.6 %all-gather.5.cloned.1.call-start = ((), (), s32[]{:S(2)}) async-start(), calls=%async_computation.4 | async-start | bytes 4587520 | tf_op jit(solution)/shard_map/all_gather | solution.py:202
  10.5 137.7 %reduce-scatter.5.cloned.1.call-start = ((), (), s32[]{:S(2)}) async-start(), calls=%async_computation.5 | async-start | bytes 9175040 | tf_op jit(solution)/shard_map/reduce_scatter | solution.py:206
  12.4 36.5 %copy-start.15 = (bf16[3,512,128]{1,2,0:T(8,128)(2,1)}, bf16[3,512,128]{1,2,0:T(8,128)(2,1)S(1)}, u32[]{:S(2)}) copy-start(bf16[3,512,128]{1,2,0:T(8,128)(2,1)S(1)} %copy.45) | copy-start | bytes 1179652
  53.3 23.3 %copy-start.13 = (bf16[128,512]{1,0:T(8,128)(2,1)S(1)}, bf16[128,512]{1,0:T(8,128)(2,1)}, u32[]{:S(2)}) copy-start(bf16[128,512]{1,0:T(8,128)(2,1)} %param.24) | copy-start | bytes 393220
  76.6 6.0 copy-start.3
  76.6 6.0 copy-start.4
  82.5 0.7 copy-start.18
  82.5 0.7 copy-start.19
  82.6 101.2 %all-gather.7.cloned.1.call-start = ((), (), s32[]{:S(2)}) async-start(), calls=%async_computation.6 | async-start | bytes 4587520 | tf_op jit(solution)/shard_map/all_gather | solution.py:211
  150.3 2.3 copy-start.20
  152.1 84.7 %reduce-scatter.7.cloned.1.call-start = ((), (), s32[]{:S(2)}) async-start(), calls=%async_computation.7 | async-start | bytes 4587520 | tf_op jit(solution)/shard_map/reduce_scatter | solution.py:213
  188.0 3.0 copy-start.5
  195.4 79.0 %all-gather.9.cloned.1.call-start = ((), (), s32[]{:S(2)}) async-start(), calls=%async_computation.8 | async-start | bytes 4587520 | tf_op jit(solution)/shard_map/all_gather | solution.py:223
  236.8 2.4 copy-start.8
  242.7 88.3 %reduce-scatter.9.cloned.1.call-start = ((), (), s32[]{:S(2)}) async-start(), calls=%async_computation.9 | async-start | bytes 4587520 | tf_op jit(solution)/shard_map/reduce_scatter | solution.py:227
  274.3 11.1 %copy-start.14 = (bf16[512,512]{1,0:T(8,128)(2,1)S(1)}, bf16[512,512]{1,0:T(8,128)(2,1)}, u32[]{:S(2)}) copy-start(bf16[512,512]{1,0:T(8,128)(2,1)} %param.26) | copy-start | bytes 1572868
  283.6 1.8 copy-start.9
  289.6 78.0 %all-gather.11.cloned.1.call-start = ((), (), s32[]{:S(2)}) async-start(), calls=%async_computation.10 | async-start | bytes 4587520 | tf_op jit(solution)/shard_map/all_gather | solution.py:234
  331.0 3.0 copy-start.2
  331.0 3.0 copy-start.10
  336.0 131.3 %reduce-scatter.11.cloned.1.call-start = ((), (), s32[]{:S(2)}) async-start(), calls=%async_computation.11 | async-start | bytes 4587520 | tf_op jit(solution)/shard_map/reduce_scatter | solution.py:238
  370.8 44.7 %copy-start.16 = (bf16[3,512,128]{1,2,0:T(8,128)(2,1)S(1)}, bf16[3,512,128]{1,2,0:T(8,128)(2,1)}, u32[]{:S(2)}) copy-start(bf16[3,512,128]{1,2,0:T(8,128)(2,1)} %copy-done.15) | copy-start | bytes 1179652
  421.2 177.8 %all-reduce.5.cloned.1.call-start = ((), (), s32[]{:S(2)}) async-start(), calls=%async_computation.12 | async-start | bytes 6291456 | tf_op jit(solution)/shard_map/psum | solution.py:246
  421.5 6.4 %copy-start.22 = (bf16[4,896,512]{2,1,0:T(8,128)(2,1)S(1)}, bf16[4,896,512]{2,1,0:T(8,128)(2,1)}, u32[]{:S(2)}) copy-start(bf16[4,896,512]{2,1,0:T(8,128)(2,1)} %all-gather.9.cloned.1.call-done) | copy-start | bytes 11010052
  427.8 8.5 %copy-start.11 = (bf16[4,896,384]{1,2,0:T(8,128)(2,1)S(1)}, bf16[4,896,384]{1,2,0:T(8,128)(2,1)}, u32[]{:S(2)}) copy-start(bf16[4,896,384]{1,2,0:T(8,128)(2,1)} %get-tuple-element.94) | copy-start | bytes 8257540
  427.8 8.5 %copy-start.21 = (bf16[4,896,512]{2,1,0:T(8,128)(2,1)S(1)}, bf16[4,896,512]{2,1,0:T(8,128)(2,1)}, u32[]{:S(2)}) copy-start(bf16[4,896,512]{2,1,0:T(8,128)(2,1)} %all-gather.5.cloned.1.call-done) | copy-start | bytes 11010052
  436.3 2.7 copy-start.7
  442.8 24.4 %copy-start.6 = (f32[4,224,512]{2,1,0:T(8,128)S(1)}, f32[4,224,512]{2,1,0:T(8,128)}, u32[]{:S(2)}) copy-start(f32[4,224,512]{2,1,0:T(8,128)} %get-tuple-element.177) | copy-start | bytes 5505028
  442.9 26.9 %copy-start.23 = (s32[4]{0:T(128)S(1)}, s32[4]{0:T(128)}, u32[]{:S(2)}) copy-start(s32[4]{0:T(128)} %param.19) | copy-start | bytes 52
  467.3 138.8 %copy-start.1 = (bf16[512,512]{1,0:T(8,128)(2,1)S(1)}, bf16[512,512]{1,0:T(8,128)(2,1)}, u32[]{:S(2)}) copy-start(bf16[512,512]{1,0:T(8,128)(2,1)} %param.28) | copy-start | bytes 1572868
  599.1 6.1 copy-start.12
  (1 other events, 0.7 us)
Sparse Core Ops, SparseCore 0:
  10.6 34.1 all-gather.4
  82.7 65.4 reduce-scatter.4
  152.2 31.4 all-gather.6
  195.5 41.2 reduce-scatter.6
  242.8 31.4 all-gather.8
  289.7 41.2 reduce-scatter.8
  336.1 31.5 all-gather.10
  421.3 41.2 reduce-scatter.10
  467.6 131.3 all-reduce.4
where the time goes:
time: 621 us; the launch traced here: 613 us
  waiting for transfers between devices  361 us (58%)
  matrix products  101 us (16%)
  blocking collectives  63.5 us (10%)
  other arithmetic  43.1 us (7%)
  local copies, waits for them, and re-layouts  27.7 us (4%)
  between operations  14.4 us (2%)
    psum x1, waiting for transfers between devices, shards(): lax.psum((qkv_grad, qvb_grad, out_grad, up_grad, upb_grad, down_grad), 'dp')  87.5 us
    reduce_scatter x1, waiting for transfers between devices, shards(): lax.psum_scatter(attn_part, 'tp', scatter_dimension=1, tiled=True)  64.9 us
    psum x1, blocking collectives, shards(): lax.psum((bias_grad, jnp.stack([gain_one, gain_two]), jnp.stack([shift_on...  41.5 us
    reduce_scatter x1, waiting for transfers between devices, shards(): lax.psum_scatter(ffn_part.astype(jnp.bfloat16), 'tp', scatter_dimension=1...  41.3 us
    reduce_scatter x1, waiting for transfers between devices, shards(): lax.psum_scatter(ffn_back_part.astype(jnp.bfloat16), 'tp', scatter_dimens...  41.2 us
    all_gather x1, waiting for transfers between devices, shards(): act_full = lax.all_gather(act_in, 'tp', axis=1, tiled=True)  31.6 us
    all_gather x1, waiting for transfers between devices, shards(): grad_two_full = lax.all_gather(grad_two_low, 'tp', axis=1, tiled=True)  31.6 us
    all_gather x1, waiting for transfers between devices, shards(): grad_one_full = lax.all_gather(grad_one_low, 'tp', axis=1, tiled=True)  31.6 us
  transfers between devices with their start and end apart: 9, of which 8 were waited for; matrix products, arithmetic and copies ran while one was open for 5% of the time, Pallas kernels for 0%

commit v1 on v0

--- a/solution.py
+++ b/solution.py
@@ -244,15 +244,14 @@
     qkv_grad = jnp.transpose(cat_grad.reshape(model_width, 3, col_width), (1, 0, 2))
     qvb_grad = jnp.stack([bcat_grad[:col_width], bcat_grad[2 * col_width :]])
     weight_totals = lax.psum((qkv_grad, qvb_grad, out_grad, up_grad, upb_grad, down_grad), "dp")
-    shared = lax.psum(
-        (
-            bias_grad,
-            jnp.stack([gain_one, gain_two]),
-            jnp.stack([shift_one, shift_two]),
-            jnp.stack([jnp.sum(grad_one, axis=(0, 1)), jnp.sum(grad_two, axis=(0, 1))]),
-        ),
-        ("dp", "tp"),
-    )
+    shared = (
+        bias_grad,
+        jnp.stack([gain_one, gain_two]),
+        jnp.stack([shift_one, shift_two]),
+        jnp.stack([jnp.sum(grad_one, axis=(0, 1)), jnp.sum(grad_two, axis=(0, 1))]),
+    )
+    for axis in ("tp", "dp"):
+        shared = lax.psum(shared, axis)
     return (
         result_rows,
         input_low,

time: 621 us -> 647 us (1.042)
  matrix products: 101 us -> 126 us
  blocking collectives: 63.5 us -> 49.9 us
  waiting for transfers between devices: 361 us -> 373 us
    reduce_scatter x1, waiting for transfers between devices: 0.01 us -> 15.8 us  [shards(): lax.psum_scatter(attn_back_part.astype(jnp.bfloat16), 'tp', scatter_dimen...]
    psum x2, blocking collectives: 63.5 us -> 49.9 us  [shards(): shared = lax.psum(shared, axis)]
    dot_general x4, matrix products: 8.49 us -> 20.3 us  [attend_back(): jnp.einsum('qhe,khe->hqk', grad_heads, v_heads, preferred_element_type=jn...]
    dot_general x8, matrix products: 9.59 us -> 20.5 us  [masked_scores(): jnp.einsum('qhe,khe->hqk', q_heads, k_heads, preferred_element_type=jnp.f...]
    unnamed x53 -> x47, local copies, waits for them, and re-layouts: 13.7 us -> 13.8 us
  transfers between devices with their start and end apart: 9 -> 9, of which waited for: 8 -> 9; matrix products, arithmetic and copies ran while one was open for 5% -> 5% of each run, Pallas kernels for 0% -> 0%
where the time goes in v1:
time: 647 us; the launch traced here: 639 us
  waiting for transfers between devices  373 us (58%)
  matrix products  126 us (19%)
  blocking collectives  49.9 us (8%)
  other arithmetic  43.2 us (7%)
  local copies, waits for them, and re-layouts  31 us (5%)
  between operations  14.4 us (2%)
    psum x1, waiting for transfers between devices, shards(): lax.psum((qkv_grad, qvb_grad, out_grad, up_grad, upb_grad, down_grad), 'dp')  83.2 us
    reduce_scatter x1, waiting for transfers between devices, shards(): lax.psum_scatter(attn_part, 'tp', scatter_dimension=1, tiled=True)  64.9 us
    psum x2, blocking collectives, shards(): shared = lax.psum(shared, axis)  49.9 us
    reduce_scatter x1, waiting for transfers between devices, shards(): lax.psum_scatter(ffn_part.astype(jnp.bfloat16), 'tp', scatter_dimension=1...  41.3 us
    reduce_scatter x1, waiting for transfers between devices, shards(): lax.psum_scatter(ffn_back_part.astype(jnp.bfloat16), 'tp', scatter_dimens...  41.2 us
    all_gather x1, waiting for transfers between devices, shards(): grad_two_full = lax.all_gather(grad_two_low, 'tp', axis=1, tiled=True)  31.6 us
    all_gather x1, waiting for transfers between devices, shards(): act_full = lax.all_gather(act_in, 'tp', axis=1, tiled=True)  31.6 us
    all_gather x1, waiting for transfers between devices, shards(): grad_one_full = lax.all_gather(grad_one_low, 'tp', axis=1, tiled=True)  31.6 us
  transfers between devices with their start and end apart: 9, of which 9 were waited for; matrix products, arithmetic and copies ran while one was open for 5% of the time, Pallas kernels for 0%

profile of v1, /device:TPU:0, one launch (start us, length us, event | category | flops | bytes accessed | tf_op | source)
XLA Modules:
  0.0 638.8 jit_solution(702686491584198822)
XLA Ops:
  13.2 31.6 %all-gather.5.cloned.1.call-done = bf16[4,896,512]{2,1,0:T(8,128)(2,1)} async-done(((bf16[4,224,512]{2,1,0:T(8,128)(2,1)}), bf16[4,896,512]{2,1,0:T(8,128)(2,1)}) %all-gather.5.cloned.1.call-update) | async-done | bytes 3670032 | tf_op jit(solution)/shard_map/all_gather | solution.py:202
  44.8 4.1 add_convert_fusion
  53.3 23.2 %while.22 = (s32[]{:T(128)}, bf16[4,896,128]{1,2,0:T(8,128)(2,1)}, f32[4,2,896]{2,1,0:T(2,128)S(1)}, bf16[4,896,128]{1,2,0:T(8,128)(2,1)S(1)}, f32[4,896]{1,0:T(...) while((s32[]{:T(128)}, bf16[4,896,128]{1,2,0:T(8,128)(2,1)}, ...), condition=%wide.region_3.4_spmd, body=%wide.region_0.3_spmd.sunk | while | flops 430423168 | bytes 22085220 | solution.py:96
  76.6 5.9 fusion.42
  83.3 64.9 %reduce-scatter.5.cloned.1.call-done = f32[4,224,512]{2,1,0:T(8,128)} async-done(((f32[4,896,512]{2,1,0:T(8,128)}), f32[4,224,512]{2,1,0:T(8,128)}) %reduce-scatter.5.cloned.1.call-update) | async-done | bytes 1835024 | tf_op jit(solution)/shard_map/reduce_scatter | solution.py:206
  152.6 31.1 %all-gather.7.cloned.1.call-done = bf16[4,896,512]{2,1,0:T(8,128)(2,1)} async-done(((bf16[4,224,512]{2,1,0:T(8,128)(2,1)}), bf16[4,896,512]{2,1,0:T(8,128)(2,1)}) %all-gather.7.cloned.1.call-update) | async-done | bytes 3670032 | tf_op jit(solution)/shard_map/all_gather | solution.py:211
  183.7 4.2 fusion.39
  190.9 4.4 convolution_convert_fusion.2
  195.5 41.3 %reduce-scatter.7.cloned.1.call-done = bf16[4,224,512]{2,1,0:T(8,128)(2,1)} async-done(((bf16[4,896,512]{2,1,0:T(8,128)(2,1)}), bf16[4,224,512]{2,1,0:T(8,128)(2,1)}) %reduce-scatter.7.cloned.1.call-update) | async-done | bytes 917520 | tf_op jit(solution)/shard_map/reduce_scatter | solution.py:213
  242.8 31.6 %all-gather.9.cloned.1.call-done = bf16[4,896,512]{2,1,0:T(8,128)(2,1)} async-done(((bf16[4,224,512]{2,1,0:T(8,128)(2,1)}), bf16[4,896,512]{2,1,0:T(8,128)(2,1)}) %all-gather.9.cloned.1.call-update) | async-done | bytes 3670032 | tf_op jit(solution)/shard_map/all_gather | solution.py:223
  274.4 9.3 %fusion.58 = (f32[512]{0:T(512)S(1)}, bf16[4,896,512]{2,1,0:T(8,128)(2,1)S(1)}) fusion(f32[4,896,512]{2,1,0:T(8,128)} %copy-done.5, f32[512]{0:T(512)S(1)} %convert_element_type.131, bf16[4,896,512]{2,1,0:T(8,128)(2,1)} %all-gather.9.cloned.1.call-done, bf16[512,512]{1,0:T(8,128)(2,1)S(1)} %copy-done), kind=kOutput, calls=%fused_computation.123 | convolution fusion | flops 1919417856 | bytes 15208448 | tf_op jit(solution)/shard_map/wvd,fd->wvf/dot_general | solution.py:144
  285.6 4.2 convolution_convert_fusion.1
  290.0 41.2 %reduce-scatter.9.cloned.1.call-done = bf16[4,224,512]{2,1,0:T(8,128)(2,1)} async-done(((bf16[4,896,512]{2,1,0:T(8,128)(2,1)}), bf16[4,224,512]{2,1,0:T(8,128)(2,1)}) %reduce-scatter.9.cloned.1.call-update) | async-done | bytes 917520 | tf_op jit(solution)/shard_map/reduce_scatter | solution.py:227
  336.2 31.6 %all-gather.11.cloned.1.call-done = bf16[4,896,512]{2,1,0:T(8,128)(2,1)} async-done(((bf16[4,224,512]{2,1,0:T(8,128)(2,1)}), bf16[4,896,512]{2,1,0:T(8,128)(2,1)}) %all-gather.11.cloned.1.call-update) | async-done | bytes 3670032 | tf_op jit(solution)/shard_map/all_gather | solution.py:234
  370.9 70.9 %while.23 = (s32[]{:T(128)}, bf16[4,896,384]{1,2,0:T(8,128)(2,1)}, bf16[4,896,128]{1,2,0:T(8,128)(2,1)}, f32[4,896]{1,0:T(4,128)S(1)}, bf16[4,896,128]{1,2,0:T(8...) while((s32[]{:T(128)}, bf16[4,896,384]{1,2,0:T(8,128)(2,1)}, ...), condition=%wide.region_17.18_spmd, body=%wide.region_15.17_spmd.sunk | while | flops 1054325888 | bytes 73458336 | solution.py:115
  372.9 3.8 fusion.127
  376.9 5.1 multiply_reduce_fusion.9
  390.6 3.8 fusion.127
  394.7 5.1 multiply_reduce_fusion.9
  408.4 3.8 fusion.127
  412.4 5.1 multiply_reduce_fusion.9
  426.1 3.8 fusion.127
  430.1 5.1 multiply_reduce_fusion.9
  441.9 5.8 convolution_convert_fusion
  448.0 6.3 fusion.31
  454.4 8.4 %convolution_bitcast_fusion = f32[512,512]{1,0:T(8,128)} fusion(bf16[4,896,512]{2,1,0:T(8,128)(2,1)S(1)} %copy-done.19, f32[4,896,512]{2,1,0:T(8,128)} %copy-done.5, f32[512]{0:T(512)S(1)} %convert_element_type.131), kind=kOutput, calls=%fused_computation.77 | convolution fusion | flops 1897398272 | bytes 12060672 | tf_op jit(solution)/shard_map/wvf,wvd->fd/dot_general | solution.py:143
  462.7 3.3 fusion.60
  467.2 3.7 convolution_bitcast_fusion.1
  473.4 15.8 %reduce-scatter.11.cloned.1.call-done = bf16[4,224,512]{2,1,0:T(8,128)(2,1)} async-done(((bf16[4,896,512]{2,1,0:T(8,128)(2,1)}), bf16[4,224,512]{2,1,0:T(8,128)(2,1)}) %reduce-scatter.11.cloned.1.call-update) | async-done | bytes 917520 | tf_op jit(solution)/shard_map/reduce_scatter | solution.py:238
  491.9 10.3 %all-reduce.2 = (f32[4,512]{1,0:T(4,128)S(1)}, f32[2,512]{1,0:T(2,128)S(1)}, f32[2,512]{1,0:T(2,128)S(1)}, f32[2,512]{1,0:T(2,128)S(1)}) all-reduce(f32[4,512]{1,0:T(4,128)S(1)} %fusion.44, f32[2,512]{1,0:T(2,128)S(1)} %pad_maximum_fusion, f32[2,512]{1,0:T(2,128)S(1)} %pad_maximum_fusion.1, ...), channel_id=1, replica_groups=mesh['dp'=8,'tp'=4] {'tp'}, use_global_device_ids=true, to_apply=%region_20.21 | all-reduce | flops 5120 | bytes 40960 | tf_op jit(solution)/shard_map/psum | solution.py:254
  502.2 39.6 %all-reduce = (f32[4,512]{1,0:T(4,128)}, f32[2,128]{1,0:T(2,128)}, f32[2,512]{1,0:T(2,128)}, f32[512]{0:T(512)}, f32[2,512]{1,0:T(2,128)}, /*index=5*/f32[2,512]{1,0:T(2,128)}) all-reduce(f32[4,512]{1,0:T(4,128)S(1)} %get-tuple-element.176, f32[2,128]{1,0:T(2,128)S(1)} %pad_maximum_fusion.4, ...), channel_id=1, replica_groups=mesh['dp'=8,'tp'=4] {'dp'}, use_global_device_ids=true, to_apply=%region_21.22 | all-reduce | flops 5888 | bytes 47104 | tf_op jit(solution)/shard_map/psum | solution.py:254
  541.8 83.2 %all-reduce.5.cloned.1.call-done = (f32[3,512,128]{2,1,0:T(8,128)}, f32[128,512]{1,0:T(8,128)}, f32[512,512]{1,0:T(8,128)}, f32[512,512]{1,0:T(8,128)}) async-done(((f32[3,512,128]{2,1,0:T(8,128)}, f32[128,512]{1,0:T(8,128)}, f32[512,512]{1,0:T(8,128)}, f32[512,512]{1,0:T(8,128)}), (f32[3,512,128]{2,1,0:T(8,128)}, f32[128,512]{1,0:T(8,128)}, f32[512,512]{1,0:T(8,128)}, ...) | async-done | bytes 3145744 | tf_op jit(solution)/shard_map/psum | solution.py:246
  (205 shorter events, 106.5 us)
Async XLA Ops:
  7.2 183.7 %copy-start = (bf16[512,512]{1,0:T(8,128)(2,1)S(1)}, bf16[512,512]{1,0:T(8,128)(2,1)}, u32[]{:S(2)}) copy-start(bf16[512,512]{1,0:T(8,128)(2,1)} %param.28) | copy-start | bytes 1572868
  7.2 37.6 %all-gather.5.cloned.1.call-start = ((), (), s32[]{:S(2)}) async-start(), calls=%async_computation.4 | async-start | bytes 4587520 | tf_op jit(solution)/shard_map/all_gather | solution.py:202
  10.5 137.7 %reduce-scatter.5.cloned.1.call-start = ((), (), s32[]{:S(2)}) async-start(), calls=%async_computation.5 | async-start | bytes 9175040 | tf_op jit(solution)/shard_map/reduce_scatter | solution.py:206
  11.7 33.1 %copy-start.13 = (bf16[3,512,128]{1,2,0:T(8,128)(2,1)}, bf16[3,512,128]{1,2,0:T(8,128)(2,1)S(1)}, u32[]{:S(2)}) copy-start(bf16[3,512,128]{1,2,0:T(8,128)(2,1)S(1)} %copy.45) | copy-start | bytes 1179652
  53.3 23.3 %copy-start.11 = (bf16[128,512]{1,0:T(8,128)(2,1)S(1)}, bf16[128,512]{1,0:T(8,128)(2,1)}, u32[]{:S(2)}) copy-start(bf16[128,512]{1,0:T(8,128)(2,1)} %param.24) | copy-start | bytes 393220
  76.6 6.0 copy-start.3
  76.6 6.0 copy-start.4
  82.6 101.2 %all-gather.7.cloned.1.call-start = ((), (), s32[]{:S(2)}) async-start(), calls=%async_computation.6 | async-start | bytes 4587520 | tf_op jit(solution)/shard_map/all_gather | solution.py:211
  152.1 84.7 %reduce-scatter.7.cloned.1.call-start = ((), (), s32[]{:S(2)}) async-start(), calls=%async_computation.7 | async-start | bytes 4587520 | tf_op jit(solution)/shard_map/reduce_scatter | solution.py:213
  187.9 3.0 copy-start.5
  195.4 79.0 %all-gather.9.cloned.1.call-start = ((), (), s32[]{:S(2)}) async-start(), calls=%async_computation.8 | async-start | bytes 4587520 | tf_op jit(solution)/shard_map/all_gather | solution.py:223
  242.7 88.5 %reduce-scatter.9.cloned.1.call-start = ((), (), s32[]{:S(2)}) async-start(), calls=%async_computation.9 | async-start | bytes 4587520 | tf_op jit(solution)/shard_map/reduce_scatter | solution.py:227
  274.4 11.2 %copy-start.12 = (bf16[512,512]{1,0:T(8,128)(2,1)S(1)}, bf16[512,512]{1,0:T(8,128)(2,1)}, u32[]{:S(2)}) copy-start(bf16[512,512]{1,0:T(8,128)(2,1)} %param.26) | copy-start | bytes 1572868
  289.7 78.0 %all-gather.11.cloned.1.call-start = ((), (), s32[]{:S(2)}) async-start(), calls=%async_computation.10 | async-start | bytes 4587520 | tf_op jit(solution)/shard_map/all_gather | solution.py:234
  331.2 3.0 copy-start.2
  331.2 3.0 copy-start.9
  336.1 153.0 %reduce-scatter.11.cloned.1.call-start = ((), (), s32[]{:S(2)}) async-start(), calls=%async_computation.11 | async-start | bytes 4587520 | tf_op jit(solution)/shard_map/reduce_scatter | solution.py:238
  376.9 5.1 slice-start
  376.9 5.1 slice-start.1
  394.6 5.1 slice-start
  394.6 5.1 slice-start.1
  412.4 5.1 slice-start
  412.4 5.1 slice-start.1
  430.1 5.1 slice-start
  430.1 5.1 slice-start.1
  447.7 177.3 %all-reduce.5.cloned.1.call-start = ((), (), s32[]{:S(2)}) async-start(), calls=%async_computation.12 | async-start | bytes 6291456 | tf_op jit(solution)/shard_map/psum | solution.py:246
  448.0 6.4 copy-start.19
  454.4 8.4 %copy-start.18 = (bf16[4,896,512]{2,1,0:T(8,128)(2,1)S(1)}, bf16[4,896,512]{2,1,0:T(8,128)(2,1)}, u32[]{:S(2)}) copy-start(bf16[4,896,512]{2,1,0:T(8,128)(2,1)} %all-gather.5.cloned.1.call-done) | copy-start | bytes 11010052
  470.9 18.2 %copy-start.6 = (f32[4,224,512]{2,1,0:T(8,128)S(1)}, f32[4,224,512]{2,1,0:T(8,128)}, u32[]{:S(2)}) copy-start(f32[4,224,512]{2,1,0:T(8,128)} %get-tuple-element.181) | copy-start | bytes 5505028
  470.9 20.7 %copy-start.20 = (s32[4]{0:T(128)S(1)}, s32[4]{0:T(128)}, u32[]{:S(2)}) copy-start(s32[4]{0:T(128)} %param.19) | copy-start | bytes 52
  489.1 142.9 %copy-start.1 = (bf16[512,512]{1,0:T(8,128)(2,1)S(1)}, bf16[512,512]{1,0:T(8,128)(2,1)}, u32[]{:S(2)}) copy-start(bf16[512,512]{1,0:T(8,128)(2,1)} %param.28) | copy-start | bytes 1572868
  625.0 6.1 copy-start.10
  (6 other events, 8.7 us)
Sparse Core Ops, SparseCore 0:
  10.6 34.1 all-gather.4
  82.7 65.4 reduce-scatter.4
  152.2 31.4 all-gather.6
  195.5 41.2 reduce-scatter.6
  242.8 31.4 all-gather.8
  289.9 41.2 reduce-scatter.8
  336.2 31.4 all-gather.10
  447.9 41.2 reduce-scatter.10
  494.2 130.7 all-reduce.4
